TPU v7x, 32 devices: a whole 2x2x4 slice. The times are simulated.
32 devices in a mesh: expert: 16 (over z, y, x), dp: 2 (over core).
Axes of the slice: x: 2, y: 2, z: 4, core: 2. Of those that a mesh axis runs over, the one named last changes fastest.
Arguments:
- tokens: bfloat16 [2048, 4096], P(('expert', 'dp')), may hold values from -6 to 6
- routes: int32 [2048, 8], P(('expert', 'dp')), may hold values from 0 to 15, all different within a row; in each aligned block of 64 rows (0 to 63, 64 to 127, ...) at most 64 rows name the same one
- gate_probs: float32 [2048, 8], P(('expert', 'dp')), may hold values from 0.05 to 0.35
- gate_w: bfloat16 [16, 4096, 768], P('expert', None, 'dp'), may hold values from -0.09375 to 0.09375
- up_w: bfloat16 [16, 4096, 768], P('expert', None, 'dp'), may hold values from -0.09375 to 0.09375
- down_w: bfloat16 [16, 768, 4096], P('expert', 'dp'), may hold values from -0.21875 to 0.21875
Outputs:
- mixed_out: bfloat16 [2048, 4096], P(('expert', 'dp'))
Inputs may be any that keep to these rules, and one draw needn't show every extreme that they name: `routes`: each token names 8 different experts. Among the 64 tokens of one device (aligned blocks of rows), no expert is named by more than 64 tokens; in some block an expert is named by exactly 64 tokens.
All inputs are finite; a program needn't handle non-finite values.
Results may differ from a plain program's by a relative error of at most 0.0057.
Values may be sent and summed in bfloat16 or wider, within the bound.
A program may use at most 192 MiB of HBM per device.

v0:
```python
import jax
import jax.numpy as jnp
from jax import lax
from jax.sharding import PartitionSpec as P


def swiglu(row_block, w_gate, w_up, w_down):
    gate_act = jnp.dot(row_block, w_gate, preferred_element_type=jnp.float32)
    up_act = jnp.dot(row_block, w_up, preferred_element_type=jnp.float32)
    hidden = (jax.nn.silu(gate_act) * up_act).astype(jnp.bfloat16)
    return jnp.dot(hidden, w_down, preferred_element_type=jnp.float32)


def apply_expert(row_block, w_gate, w_up, w_down):
    return swiglu(row_block, w_gate, w_up, w_down)


def body(tokens, routes, gate_probs, gate_w, up_w, down_w):
    experts = lax.axis_size("expert")
    tok_count, model_width = tokens.shape
    top_count = routes.shape[1]
    capacity = 2 * tok_count * top_count // experts
    expert_ids = jnp.arange(experts, dtype=jnp.int32)
    named_hits = jnp.sum((routes[:, :, None] == expert_ids).astype(jnp.int32), axis=1)
    before = jnp.cumsum(named_hits, axis=0) - named_hits
    slot_index = jnp.take_along_axis(before, routes, axis=1)
    target = routes * capacity + slot_index
    buffer_rows = jnp.arange(experts * capacity, dtype=jnp.int32)
    placer = jnp.sum(
        (target[None, :, :] == buffer_rows[:, None, None]).astype(jnp.float32), axis=2
    ).astype(jnp.bfloat16)
    outgoing = jnp.dot(placer, tokens, preferred_element_type=jnp.float32).astype(jnp.bfloat16)
    outgoing = outgoing.reshape(experts, capacity, model_width)
    present = (
        jnp.sum(placer.astype(jnp.float32), axis=1).astype(jnp.bfloat16).reshape(experts, capacity)
    )
    w_gate = gate_w[0]
    w_up = up_w[0]
    w_down = down_w[0]
    row_block = lax.all_to_all(outgoing, "expert", split_axis=0, concat_axis=0, tiled=True)
    flag_block = lax.all_to_all(present, "expert", split_axis=0, concat_axis=0, tiled=True)
    source_count = row_block.shape[0]
    item_count = row_block.shape[1]
    flat_rows = row_block.reshape(-1, model_width)
    flat_flags = flag_block.reshape(-1)
    both_rows = lax.all_gather(flat_rows, "dp", axis=0, tiled=True)
    partial_out = apply_expert(both_rows, w_gate, w_up, w_down)
    result = lax.psum_scatter(partial_out, "dp", scatter_dimension=0, tiled=True)
    masked = result * flat_flags.astype(jnp.float32)[:, None]
    answered = masked.astype(jnp.bfloat16).reshape(source_count, item_count, model_width)
    returned = lax.all_to_all(answered, "expert", split_axis=0, concat_axis=0, tiled=True)
    picked = returned.reshape(experts * capacity, model_width)[target]
    mixed_out = jnp.einsum(
        "tk,tkd->td", gate_probs, picked.astype(jnp.float32), precision=lax.Precision.HIGHEST
    )
    return mixed_out.astype(jnp.bfloat16)


def solution(mesh):
    return jax.shard_map(
        body,
        mesh=mesh,
        in_specs=(
            P(("expert", "dp"), None),
            P(("expert", "dp"), None),
            P(("expert", "dp"), None),
            P("expert", None, "dp"),
            P("expert", None, "dp"),
            P("expert", "dp", None),
        ),
        out_specs=P(("expert", "dp"), None),
        check_vma=False,
    )
```

profile of v0, /device:TPU:8, one launch (start us, length us, event | category | flops | bytes accessed | tf_op | source)
XLA Modules:
  0.0 547.1 jit_solution(6625969062759637655)
XLA Ops:
  6.5 0.8 bitcast_or_fusion
  7.4 0.8 convert_reduce_fusion.2
  8.2 0.1 copy.36
  8.3 0.1 copy.38
  8.4 0.1 reshape.50
  8.5 0.1 reduce_window_sum.11
  8.6 3.8 gather_fusion.1
  12.3 0.1 reshape.53
  12.4 0.1 copy.39
  12.5 0.1 copy.40
  12.6 0.7 convert_reduce_fusion
  13.3 3.4 convolution_convert_fusion
  16.7 190.1 %all_to_all.20 = bf16[16,64,4096]{2,1,0:T(8,128)(2,1)} all-to-all(bf16[16,64,4096]{2,1,0:T(8,128)(2,1)S(1)} %bitcast.32), channel_id=1, replica_groups=mesh['expert'=16,'dp'=2] {'expert'}, dimensions={0} | all-to-all | bytes 16777216 | tf_op jit(solution)/shard_map/all_to_all | solution.py:40
  206.8 0.0 all-gather.2.cloned.1.call-update
  206.9 0.0 reduce-scatter.2.cloned.1.call-start
  206.9 28.9 %all-gather.2.cloned.1.call-done = bf16[2048,4096]{1,0:T(8,128)(2,1)} async-done(((bf16[1024,4096]{1,0:T(8,128)(2,1)}), bf16[2048,4096]{1,0:T(8,128)(2,1)}) %all-gather.2.cloned.1.call-update) | async-done | bytes 16777232 | tf_op jit(solution)/shard_map/all_gather | solution.py:46
  235.9 13.0 %fusion.5 = f32[2048,384]{1,0:T(8,128)S(1)} fusion(bf16[2048,4096]{1,0:T(8,128)(2,1)} %all-gather.2.cloned.1.call-done, bf16[1,4096,384]{2,1,0:T(8,128)(2,1)} %param.9), kind=kOutput, calls=%fused_computation.10 | convolution fusion | flops 6442450944 | bytes 23068672 | tf_op jit(solution)/shard_map/dot_general | solution.py:8
  248.9 12.5 %fusion.7 = bf16[2048,384]{1,0:T(8,128)(2,1)S(1)} fusion(bf16[2048,4096]{1,0:T(8,128)(2,1)} %all-gather.2.cloned.1.call-done, bf16[1,4096,384]{2,1,0:T(8,128)(2,1)S(1)} %copy-done.4, f32[2048,384]{1,0:T(8,128)S(1)} %fusion.5), kind=kOutput, calls=%fused_computation.12 | convolution fusion | flops 6447169536 | bytes 24641536 | tf_op jit(solution)/shard_map/dot_general | solution.py:9
  261.4 14.5 %fusion.2 = f32[2048,4096]{1,0:T(8,128)} fusion(bf16[2048,384]{1,0:T(8,128)(2,1)S(1)} %fusion.7, bf16[1,384,4096]{2,1,0:T(8,128)(2,1)S(1)} %copy-done), kind=kOutput, calls=%fused_computation.7 | convolution fusion | flops 6442450944 | bytes 38273024 | tf_op jit(solution)/shard_map/dot_general | solution.py:11
  276.0 0.1 all_to_all.16
  276.1 12.7 %all_to_all.21 = bf16[16,1,64]{2,1,0:T(2,128)(2,1)S(1)} all-to-all(bf16[16,1,64]{2,1,0:T(2,128)(2,1)S(1)} %all_to_all.16), channel_id=1, replica_groups=mesh['expert'=16,'dp'=2] {'expert'}, dimensions={0} | all-to-all | bytes 4096 | tf_op jit(solution)/shard_map/all_to_all | solution.py:41
  288.8 0.1 reshape.41
  288.8 33.6 %reduce-scatter.2.cloned.1.call-done = f32[1024,4096]{1,0:T(8,128)} async-done(((f32[2048,4096]{1,0:T(8,128)}), f32[1024,4096]{1,0:T(8,128)}) %reduce-scatter.2.cloned.1.call-update) | async-done | bytes 16777232 | tf_op jit(solution)/shard_map/reduce_scatter | solution.py:48
  322.4 9.3 %multiply_convert_fusion = bf16[1024,4096]{1,0:T(8,128)(2,1)} fusion(f32[1024,4096]{1,0:T(8,128)} %reduce-scatter.2.cloned.1.call-done, f32[1024]{0:T(1024)S(1)} %reshape.41), kind=kLoop, calls=%fused_computation.2 | loop fusion | flops 8388608 | bytes 25169920 | tf_op jit(solution)/shard_map/convert_element_type | solution.py:50
  331.7 7.1 %all-to-all-start.2 = ((bf16[16,64,4096]{2,1,0:T(8,128)(2,1)}), bf16[16,64,4096]{2,1,0:T(8,128)(2,1)}, u32[]{:S(2)}, u32[]{:S(2)}) async-start(bf16[16,64,4096]{2,1,0:T(8,128)(2,1)} %bitcast.33), calls=%async_computation.3 | async-start | bytes 16777216 | tf_op jit(solution)/shard_map/all_to_all | solution.py:51
  338.9 0.1 copy.42
  338.9 0.1 reshape.44
  339.0 0.1 copy.43
  339.1 180.9 %all-to-all-done.2 = bf16[16,64,4096]{2,1,0:T(8,128)(2,1)} async-done(((bf16[16,64,4096]{2,1,0:T(8,128)(2,1)}), bf16[16,64,4096]{2,1,0:T(8,128)(2,1)}, u32[]{:S(2)}, u32[]{:S(2)}) %all-to-all-start.2) | async-done | bytes 8388640 | tf_op jit(solution)/shard_map/all_to_all | solution.py:51
  520.0 13.2 %gather_fusion = bf16[512,4096]{1,0:T(8,128)(2,1)} fusion(bf16[1024,4096]{1,0:T(8,128)(2,1)} %bitcast.7, s32[1024]{0:T(1024)S(1)} %pad_clamp_fusion), kind=kCustom, calls=%fused_computation | custom fusion | bytes 8390656 | tf_op jit(solution)/shard_map/gather | solution.py:52
  533.2 5.7 %fusion = bf16[64,1,4096]{2,1,0:T(2,128)(2,1)S(1)} fusion(f32[64,8,1]{1,2,0:T(1,128)S(1)} %copy.43, bf16[512,4096]{1,0:T(8,128)(2,1)} %gather_fusion), kind=kOutput, calls=%fused_computation.4 | convolution fusion | flops 25165824 | bytes 4720640 | tf_op jit(solution)/shard_map/tk,tkd->td/dot_general | solution.py:53
  538.9 1.4 copy.46
  (17 shorter events, 0.1 us)
Async XLA Ops:
  6.5 254.9 %copy-start = (bf16[1,384,4096]{2,1,0:T(8,128)(2,1)S(1)}, bf16[1,384,4096]{2,1,0:T(8,128)(2,1)}, u32[]{:S(2)}) copy-start(bf16[1,384,4096]{2,1,0:T(8,128)(2,1)} %param.11) | copy-start | bytes 9437188
  6.5 229.3 %all-gather.2.cloned.1.call-start = ((), (), s32[]{:S(2)}) async-start(), calls=%async_computation.4 | async-start | bytes 25165824 | tf_op jit(solution)/shard_map/all_gather | solution.py:46
  8.6 3.9 copy-start.2
  206.9 115.5 %reduce-scatter.2.cloned.1.call-start = ((), (), s32[]{:S(2)}) async-start(), calls=%async_computation.5 | async-start | bytes 50331648 | tf_op jit(solution)/shard_map/reduce_scatter | solution.py:48
  235.9 13.0 %copy-start.4 = (bf16[1,4096,384]{2,1,0:T(8,128)(2,1)S(1)}, bf16[1,4096,384]{2,1,0:T(8,128)(2,1)}, u32[]{:S(2)}) copy-start(bf16[1,4096,384]{2,1,0:T(8,128)(2,1)} %param.10) | copy-start | bytes 9437188
  331.7 7.3 %copy-start.3 = (f32[64,8]{0,1:T(8,128)S(1)}, f32[64,8]{0,1:T(8,128)}, u32[]{:S(2)}) copy-start(f32[64,8]{0,1:T(8,128)} %param.8) | copy-start | bytes 6148
  331.7 188.3 %all-to-all-start.2 = ((bf16[16,64,4096]{2,1,0:T(8,128)(2,1)}), bf16[16,64,4096]{2,1,0:T(8,128)(2,1)}, u32[]{:S(2)}, u32[]{:S(2)}) async-start(bf16[16,64,4096]{2,1,0:T(8,128)(2,1)} %bitcast.33), calls=%async_computation.3 | async-start | bytes 16777216 | tf_op jit(solution)/shard_map/all_to_all | solution.py:51
  520.0 20.3 %copy-start.1 = (bf16[1,384,4096]{2,1,0:T(8,128)(2,1)S(1)}, bf16[1,384,4096]{2,1,0:T(8,128)(2,1)}, u32[]{:S(2)}) copy-start(bf16[1,384,4096]{2,1,0:T(8,128)(2,1)} %param.11) | copy-start | bytes 9437188
Sparse Core Ops, SparseCore 0:
  207.0 28.8 all-gather.1
  276.1 46.3 reduce-scatter.1
where the time goes:
time: 557 us; the launch traced here: 547 us
  waiting for transfers between devices  243 us (44%)
  blocking collectives  203 us (36%)
  matrix products  49.1 us (9%)
  local copies, waits for them, and re-layouts  19.2 us (3%)
  between operations  13.5 us (2%)
  other arithmetic  11.9 us (2%)
  starting transfers between devices  7.17 us (1%)
    all_to_all x1, blocking collectives, body(): lax.all_to_all(outgoing, 'expert', split_axis=0, concat_axis=0, tiled=True)  190 us
    all_to_all x1, waiting for transfers between devices, body(): lax.all_to_all(answered, 'expert', split_axis=0, concat_axis=0, tiled=True)  181 us
    reduce_scatter x1, waiting for transfers between devices, body(): lax.psum_scatter(partial_out, 'dp', scatter_dimension=0, tiled=True)  33.6 us
    all_gather x1, waiting for transfers between devices, body(): both_rows = lax.all_gather(flat_rows, 'dp', axis=0, tiled=True)  28.9 us
    dot_general x1, matrix products, swiglu(): return jnp.dot(hidden, w_down, preferred_element_type=jnp.float32)  14.5 us
    gather x1, local copies, waits for them, and re-layouts, body(): picked = returned.reshape(experts * capacity, model_width)[target]  13.2 us
    dot_general x1, matrix products, swiglu(): gate_act = jnp.dot(row_block, w_gate, preferred_element_type=jnp.float32)  13 us
    all_to_all x1, blocking collectives, body(): lax.all_to_all(present, 'expert', split_axis=0, concat_axis=0, tiled=True)  12.7 us
  transfers between devices with their start and end apart: 3, of which 3 were waited for; matrix products, arithmetic and copies ran while one was open for 0% of the time, Pallas kernels for 0%

commit v1 on v0

--- a/solution.py
+++ b/solution.py
@@ -15,7 +15,7 @@
     return swiglu(row_block, w_gate, w_up, w_down)
 
 
-def body(tokens, routes, gate_probs, gate_w, up_w, down_w):
+def exchange_body(tokens, routes, gate_probs, gate_w, up_w, down_w):
     experts = lax.axis_size("expert")
     tok_count, model_width = tokens.shape
     top_count = routes.shape[1]
@@ -56,6 +56,32 @@
     return mixed_out.astype(jnp.bfloat16)
 
 
+def gather_body(tokens, routes, gate_probs, gate_w, up_w, down_w):
+    experts = lax.axis_size("expert")
+    me = lax.axis_index("expert")
+    expert_ids = jnp.arange(experts, dtype=jnp.int32)
+    named = routes[:, :, None] == expert_ids
+    spread = jnp.sum(jnp.where(named, gate_probs[:, :, None], 0.0), axis=1)
+    w_gate = lax.all_gather(gate_w[0], "dp", axis=1, tiled=True)
+    w_up = lax.all_gather(up_w[0], "dp", axis=1, tiled=True)
+    w_down = lax.all_gather(down_w[0], "dp", axis=0, tiled=True)
+    all_rows = lax.all_gather(tokens, "expert", axis=0, tiled=True)
+    all_spread = lax.all_gather(spread, "expert", axis=0, tiled=True)
+    weight = lax.dynamic_slice_in_dim(all_spread, me, 1, axis=1)
+    out = apply_expert(all_rows, w_gate, w_up, w_down) * weight
+    return lax.psum_scatter(
+        out.astype(jnp.bfloat16), "expert", scatter_dimension=0, tiled=True
+    )
+
+
+def body(tokens, routes, *others):
+    tok_count, top_count = routes.shape
+    capacity = 2 * tok_count * top_count // lax.axis_size("expert")
+    if capacity >= tok_count:
+        return gather_body(tokens, routes, *others)
+    return exchange_body(tokens, routes, *others)
+
+
 def solution(mesh):
     return jax.shard_map(
         body,

time: 557 us -> 379 us (0.68); the launches traced: 547 us -> 376 us
  blocking collectives: 203 us -> 35.3 us
  waiting for transfers between devices: 243 us -> 293 us
  local copies, waits for them, and re-layouts: 19.2 us -> 0.16 us
  matrix products: 49.1 us -> 34.2 us
  other arithmetic: 11.9 us -> 0.02 us
  starting transfers between devices: 7.17 us -> 0.15 us
    all_to_all x2 -> x0, blocking collectives: 203 us -> none  [the longest x1 190 us: body(): lax.all_to_all(outgoing, 'expert', split_axis=0, concat_axis=0, tiled=True)]
    all_to_all x1 -> x0, waiting for transfers between devices: 181 us -> none  [body(): lax.all_to_all(answered, 'expert', split_axis=0, concat_axis=0, tiled=True)]
    reduce_scatter x1, waiting for transfers between devices: 33.6 us -> 179 us  [gather_body(): lax.psum_scatter(out.astype(jnp.bfloat16), 'expert', scatter_dimension=0,...]
    all_gather x1 -> x4, waiting for transfers between devices: 28.9 us -> 112 us  [the longest x1 97.5 us: gather_body(): all_rows = lax.all_gather(tokens, 'expert', axis=0, tiled=True)]
    all_gather x0 -> x1, blocking collectives: none -> 35.3 us  [gather_body(): all_spread = lax.all_gather(spread, 'expert', axis=0, tiled=True)]
    gather x6 -> x0, local copies, waits for them, and re-layouts: 17.3 us -> none  [the longest x1 13.2 us: body(): picked = returned.reshape(experts * capacity, model_width)[target]]
    convert_element_type x2 -> x0, other arithmetic: 9.35 us -> none  [the longest x1 9.32 us: body(): masked.astype(jnp.bfloat16).reshape(source_count, item_count, model_width)]
    dot_general x2 -> x0, matrix products: 9.11 us -> none  [the longest x1 5.7 us: body(): jnp.einsum('tk,tkd->td', gate_probs, picked.astype(jnp.float32), precisio...]
  transfers between devices with their start and end apart: 3 -> 5, of which waited for: 3 -> 4; matrix products, arithmetic and copies ran while one was open for 0% -> 6% of each run, Pallas kernels for 0% -> 0%
where the time goes in v1:
time: 379 us; the launch traced here: 376 us
  waiting for transfers between devices  293 us (77%)
  blocking collectives  35.3 us (9%)
  matrix products  34.2 us (9%)
  between operations  13.2 us (3%)
    reduce_scatter x1, waiting for transfers between devices, gather_body(): lax.psum_scatter(out.astype(jnp.bfloat16), 'expert', scatter_dimension=0,...  179 us
    all_gather x1, waiting for transfers between devices, gather_body(): all_rows = lax.all_gather(tokens, 'expert', axis=0, tiled=True)  97.5 us
    all_gather x1, blocking collectives, gather_body(): all_spread = lax.all_gather(spread, 'expert', axis=0, tiled=True)  35.3 us
    dot_general x1, matrix products, swiglu(): gate_act = jnp.dot(row_block, w_gate, preferred_element_type=jnp.float32)  12.1 us
    dot_general x1, matrix products, swiglu(): return jnp.dot(hidden, w_down, preferred_element_type=jnp.float32)  11.2 us
    dot_general x1, matrix products, swiglu(): up_act = jnp.dot(row_block, w_up, preferred_element_type=jnp.float32)  10.9 us
  transfers between devices with their start and end apart: 5, of which 4 were waited for; matrix products, arithmetic and copies ran while one was open for 6% of the time, Pallas kernels for 0%

profile of v1, /device:TPU:8, one launch (start us, length us, event | category | flops | bytes accessed | tf_op | source)
XLA Modules:
  0.0 375.9 jit_solution(5264166704728528419)
XLA Ops:
  6.5 0.0 copy-start.1
  6.5 0.0 copy-start
  6.5 0.0 all-gather.13.cloned.1.call-start
  6.5 0.7 all-gather.13.cloned.1.call-update
  7.3 0.0 all-gather.9.cloned.1.call-start
  7.3 0.7 all-gather.9.cloned.1.call-update
  8.0 0.0 all-gather.11.cloned.1.call-start
  8.1 0.7 all-gather.11.cloned.1.call-update
  8.7 0.0 all-gather.15.cloned.1.call-start
  8.8 0.5 all-gather.15.cloned.1.call-update
  9.3 0.0 reduce-scatter.2.cloned.1.call-start
  9.4 0.0 copy-done.1
  9.4 0.0 copy-done
  9.4 35.3 %all-gather.3 = f32[16,64,16]{1,2,0:T(8,128)S(1)} all-gather(f32[1,64,16]{1,2,0:T(8,128)S(1)} %bitcast.18), channel_id=1, replica_groups=mesh['expert'=16,'dp'=2] {'expert'}, dimensions={0}, use_global_device_ids=true | all-gather | bytes 69632 | tf_op jit(solution)/shard_map/all_gather | solution.py:69
  44.8 0.1 reshape.6
  44.9 0.0 all-gather.13.cloned.1.call-done
  44.9 97.5 %all-gather.9.cloned.1.call-done = bf16[1024,4096]{1,0:T(8,128)(2,1)} async-done(((bf16[64,4096]{1,0:T(8,128)(2,1)}), bf16[1024,4096]{1,0:T(8,128)(2,1)}) %all-gather.9.cloned.1.call-update) | async-done | bytes 8388624 | tf_op jit(solution)/shard_map/all_gather | solution.py:68
  142.4 10.9 %fusion.1 = f32[1024,768]{1,0:T(8,128)S(1)} fusion(bf16[1024,4096]{1,0:T(8,128)(2,1)} %all-gather.9.cloned.1.call-done, bf16[1,4096,768]{2,1,0:T(8,128)(2,1)} %all-gather.13.cloned.1.call-done), kind=kOutput, calls=%fused_computation.2 | convolution fusion | flops 6442450944 | bytes 17825792 | tf_op jit(solution)/shard_map/dot_general | solution.py:9
  153.3 6.9 %all-gather.11.cloned.1.call-done = bf16[1,4096,768]{2,1,0:T(8,128)(2,1)} async-done(((bf16[1,4096,384]{2,1,0:T(8,128)(2,1)}), bf16[1,4096,768]{2,1,0:T(8,128)(2,1)}) %all-gather.11.cloned.1.call-update) | async-done | bytes 6291472 | tf_op jit(solution)/shard_map/all_gather | solution.py:65
  160.2 12.1 %multiply_convert_fusion.1 = bf16[1024,768]{1,0:T(8,128)(2,1)} fusion(f32[1024,768]{1,0:T(8,128)S(1)} %fusion.1, bf16[1024,4096]{1,0:T(8,128)(2,1)} %all-gather.9.cloned.1.call-done, bf16[1,4096,768]{2,1,0:T(8,128)(2,1)} %all-gather.11.cloned.1.call-done), kind=kOutput, calls=%fused_computation.6 | convolution fusion | flops 6447169536 | bytes 19398656 | tf_op jit(solution)/shard_map/dot_general | solution.py:8
  172.3 7.2 %all-gather.15.cloned.1.call-done = bf16[1,768,4096]{2,1,0:T(8,128)(2,1)} async-done(((bf16[1,384,4096]{2,1,0:T(8,128)(2,1)}), bf16[1,768,4096]{2,1,0:T(8,128)(2,1)}) %all-gather.15.cloned.1.call-update) | async-done | bytes 6291472 | tf_op jit(solution)/shard_map/all_gather | solution.py:67
  179.5 11.2 %multiply_convert_fusion = bf16[1024,4096]{1,0:T(8,128)(2,1)} fusion(f32[1024]{0:T(1024)S(1)} %bitcast.19, bf16[1024,768]{1,0:T(8,128)(2,1)} %multiply_convert_fusion.1, bf16[1,768,4096]{2,1,0:T(8,128)(2,1)} %all-gather.15.cloned.1.call-done), kind=kOutput, calls=%fused_computation | convolution fusion | flops 6450839552 | bytes 16257024 | tf_op jit(solution)/shard_map/dot_general | solution.py:11
  190.7 0.0 reduce-scatter.2.cloned.1.call-update
  190.7 178.6 %reduce-scatter.2.cloned.1.call-done = bf16[64,4096]{1,0:T(8,128)(2,1)} async-done(((bf16[1024,4096]{1,0:T(8,128)(2,1)}), bf16[64,4096]{1,0:T(8,128)(2,1)}) %reduce-scatter.2.cloned.1.call-update) | async-done | bytes 524304 | tf_op jit(solution)/shard_map/reduce_scatter | solution.py:72
  (3 shorter events, 0.1 us)
Async XLA Ops:
  6.5 2.8 copy-start.1
  6.5 2.8 copy-start
  6.5 38.4 %all-gather.13.cloned.1.call-start = ((), (), s32[]{:S(2)}) async-start(), calls=%async_computation.4 | async-start | bytes 9437184 | tf_op jit(solution)/shard_map/all_gather | solution.py:66
  7.3 135.1 %all-gather.9.cloned.1.call-start = ((), (), s32[]{:S(2)}) async-start(), calls=%async_computation.1 | async-start | bytes 8912896 | tf_op jit(solution)/shard_map/all_gather | solution.py:68
  8.0 152.2 %all-gather.11.cloned.1.call-start = ((), (), s32[]{:S(2)}) async-start(), calls=%async_computation.3 | async-start | bytes 9437184 | tf_op jit(solution)/shard_map/all_gather | solution.py:65
  8.7 170.8 %all-gather.15.cloned.1.call-start = ((), (), s32[]{:S(2)}) async-start(), calls=%async_computation.5 | async-start | bytes 9437184 | tf_op jit(solution)/shard_map/all_gather | solution.py:67
  9.3 360.1 %reduce-scatter.2.cloned.1.call-start = ((), (), s32[]{:S(2)}) async-start(), calls=%async_computation.2 | async-start | bytes 8912896 | tf_op jit(solution)/shard_map/reduce_scatter | solution.py:72
Sparse Core Ops, SparseCore 0:
  8.9 17.9 all-gather.12
  29.7 112.6 all-gather.8
  143.9 16.1 all-gather.10
  161.6 17.9 all-gather.14
  190.9 178.4 reduce-scatter.1

commit v2 on v0

--- a/solution.py
+++ b/solution.py
@@ -1,6 +1,8 @@
 import jax
 import jax.numpy as jnp
 from jax import lax
+from jax.experimental import pallas as pl
+from jax.experimental.pallas import tpu as pltpu
 from jax.sharding import PartitionSpec as P
 
 
@@ -15,7 +17,7 @@
     return swiglu(row_block, w_gate, w_up, w_down)
 
 
-def body(tokens, routes, gate_probs, gate_w, up_w, down_w):
+def exchange_body(tokens, routes, gate_probs, gate_w, up_w, down_w):
     experts = lax.axis_size("expert")
     tok_count, model_width = tokens.shape
     top_count = routes.shape[1]
@@ -56,6 +58,388 @@
     return mixed_out.astype(jnp.bfloat16)
 
 
+MESH = pl.DeviceIdType.MESH
+DEPTH = 4
+TAG = 128
+
+
+def fused_kernel(
+    rows_ref, gate_ref, up_ref, down_ref, out_ref,
+    xa, xb, w_in, w_out, hidden, stay, pass_on, leave, got_third, got_second, rise, fall,
+    gather_send, gather_recv, reduce_send, reduce_recv, weight_sem,
+):
+    tok = rows_ref.shape[0]
+    half = xb.shape[2]
+    unit = gate_ref.shape[1]
+    me = lax.axis_index("expert")
+    core = lax.axis_index("dp")
+    z = me // 4
+    y = (me // 2) % 2
+    x = me % 2
+    above, below = {"expert": me + 4}, {"expert": me - 4}
+    across_y, across_x = {"expert": me + 2 - 4 * y}, {"expert": me + 1 - 2 * x}
+    sibling = {"dp": 1 - core}
+    second = (across_y, across_x)
+    third = (across_x, across_y)
+    feats = (xa, xb)
+
+    def when(cond, fn):
+        pl.when(cond)(fn)
+
+    def piece(zz):
+        if isinstance(zz, int):
+            return pl.ds(zz * tok, tok)
+        return pl.ds(pl.multiple_of(zz * tok, tok), tok)
+
+    def remote(src, dst, send, recv, device):
+        return pltpu.make_async_remote_copy(
+            src_ref=src, dst_ref=dst, send_sem=send, recv_sem=recv,
+            device_id=device, device_id_type=MESH,
+        )
+
+    barrier = pltpu.get_barrier_semaphore()
+    for device in (across_y, across_x, sibling):
+        pl.semaphore_signal(barrier, inc=1, device_id=device, device_id_type=MESH)
+
+    @pl.when(z < DEPTH - 1)
+    def _():
+        pl.semaphore_signal(barrier, inc=1, device_id=above, device_id_type=MESH)
+
+    @pl.when(z > 0)
+    def _():
+        pl.semaphore_signal(barrier, inc=1, device_id=below, device_id_type=MESH)
+
+    xa[0, piece(z), :] = rows_ref[:, : TAG + half]
+    xb[0, piece(z), :] = rows_ref[:, TAG + half :]
+
+    edge = jnp.logical_or(z == 0, z == DEPTH - 1)
+
+    @pl.when(edge)
+    def _():
+        pl.semaphore_wait(barrier, 4)
+
+    @pl.when(jnp.logical_not(edge))
+    def _():
+        pl.semaphore_wait(barrier, 5)
+
+    def gather(f, src_kind, dst_kind, zz, slot, device):
+        return remote(
+            feats[f].at[src_kind, piece(zz)], feats[f].at[dst_kind, piece(zz)],
+            gather_send.at[f, slot + zz], gather_recv.at[f, dst_kind * DEPTH + zz], device,
+        )
+
+    def climb(f, zz):
+        return gather(f, 0, 0, zz, 0, above)
+
+    def sink(f, zz):
+        return gather(f, 0, 0, zz, 4, below)
+
+    def own_second(f, zz):
+        return gather(f, 0, 1, zz, 8, second[f])
+
+    def own_third(f, zz):
+        return gather(f, 0, 2, zz, 12, third[f])
+
+    def second_third(f, zz):
+        return gather(f, 1, 3, zz, 16, third[f])
+
+    for f in range(2):
+        when(z < DEPTH - 1, lambda f=f: climb(f, z).start())
+        when(z > 0, lambda f=f: sink(f, z).start())
+        own_second(f, z).start()
+    for f in range(2):
+        own_third(f, z).start()
+
+    pairs = (
+        (gate_ref, w_in.at[:, pl.ds(0, unit)], w_in.at[:, pl.ds(unit, unit)]),
+        (up_ref, w_in.at[:, pl.ds(2 * unit, unit)], w_in.at[:, pl.ds(3 * unit, unit)]),
+        (down_ref, w_out.at[pl.ds(0, unit)], w_out.at[pl.ds(unit, unit)]),
+    )
+    swaps = []
+    for i, (src, mine, other) in enumerate(pairs):
+        local = pltpu.make_async_copy(src, mine, weight_sem.at[3 * i])
+        swap = remote(src, other, weight_sem.at[3 * i + 1], weight_sem.at[3 * i + 2], sibling)
+        local.start()
+        swap.start()
+        swaps.append((local, swap))
+
+    def relay_second(zz):
+        for f in range(2):
+            own_second(f, zz).wait_recv()
+            second_third(f, zz).start()
+
+    for k in range(1, DEPTH):
+        def from_below(k=k):
+            zz = z - k
+            for f in range(2):
+                climb(f, zz).wait_recv()
+                when(z < DEPTH - 1, lambda f=f: climb(f, zz).start())
+                own_second(f, zz).start()
+                own_third(f, zz).start()
+
+        def from_above(k=k):
+            zz = z + k
+            for f in range(2):
+                sink(f, zz).wait_recv()
+                when(z > 0, lambda f=f: sink(f, zz).start())
+                own_second(f, zz).start()
+                own_third(f, zz).start()
+
+        when(z >= k, from_below)
+        when(z + k < DEPTH, from_above)
+        if k == 1:
+            relay_second(z)
+        else:
+            when(z >= k - 1, lambda k=k: relay_second(z - k + 1))
+            when(z + k - 1 < DEPTH, lambda k=k: relay_second(z + k - 1))
+
+    def expert(kind_a, kind_b, targets):
+        lane = lax.broadcasted_iota(jnp.int32, (DEPTH * tok, TAG), 1)
+        mine = jnp.logical_or(lane == me, lane == me + 16)
+        tags = xa[kind_a, :, :TAG].astype(jnp.float32)
+        weight = jnp.sum(jnp.where(mine, tags, 0.0), axis=1, keepdims=True)
+
+        def hidden_tile(j, carry):
+            cols = pl.multiple_of(j * 256, 256)
+            gate_cols, up_cols = pl.ds(cols, 256), pl.ds(2 * unit + cols, 256)
+
+            def project(columns):
+                return jnp.dot(
+                    xa[kind_a, :, TAG:], w_in[:half, columns], preferred_element_type=jnp.float32
+                ) + jnp.dot(
+                    xb[kind_b], w_in[half:, columns], preferred_element_type=jnp.float32
+                )
+
+            gate_act = project(gate_cols)
+            up_act = project(up_cols)
+            act = gate_act / (1.0 + jnp.exp(-gate_act)) * up_act
+            hidden[:, gate_cols] = act.astype(jnp.bfloat16)
+            return carry
+
+        lax.fori_loop(0, 2 * unit // 256, hidden_tile, 0)
+        for f in range(2):
+            target = targets[f]
+
+            def out_tile(j, carry, f=f, target=target):
+                cols = pl.multiple_of(j * 512, 512)
+                val = jnp.dot(
+                    hidden[...], w_out[:, pl.ds(f * half + cols, 512)],
+                    preferred_element_type=jnp.float32,
+                )
+                target[:, pl.ds(cols, 512)] = (val * weight).astype(target.dtype)
+                return carry
+
+            lax.fori_loop(0, half // 512, out_tile, 0)
+
+    order = (3, 0, 2, 1)
+
+    def leave_third(f, zz):
+        return remote(
+            leave.at[f, 0, piece(zz)], got_third.at[f, 0, piece(zz)],
+            reduce_send.at[f, zz], reduce_recv.at[f, zz], third[f],
+        )
+
+    def leave_both(f, zz):
+        return remote(
+            leave.at[f, 1, piece(zz)], got_third.at[f, 1, piece(zz)],
+            reduce_send.at[f, 4 + zz], reduce_recv.at[f, 4 + zz], third[f],
+        )
+
+    def leave_second(f, zz):
+        return remote(
+            got_third.at[f, 1, piece(zz)], got_second.at[f, piece(zz)],
+            reduce_send.at[f, 8 + zz], reduce_recv.at[f, 8 + zz], second[f],
+        )
+
+    def rising(f, zz):
+        return remote(
+            rise.at[f, piece(zz)], rise.at[f, piece(zz)],
+            reduce_send.at[f, 12 + zz], reduce_recv.at[f, 12 + zz], above,
+        )
+
+    def falling(f, zz):
+        return remote(
+            fall.at[f, piece(zz)], fall.at[f, piece(zz)],
+            reduce_send.at[f, 16 + zz], reduce_recv.at[f, 16 + zz], below,
+        )
+
+    for local, swap in swaps:
+        local.wait()
+        swap.wait_recv()
+    expert(0, 0, (stay.at[0], stay.at[1]))
+    when(z >= 3, lambda: relay_second(z - 3))
+    when(z + 3 < DEPTH, lambda: relay_second(z + 3))
+
+    for zz in range(DEPTH):
+        own_third(0, zz).wait_recv()
+    expert(2, 1, (leave.at[0, 0], pass_on.at[1]))
+    for zz in order:
+        leave_third(0, zz).start()
+    for zz in range(DEPTH):
+        own_third(1, zz).wait_recv()
+    expert(1, 2, (pass_on.at[0], leave.at[1, 0]))
+    for zz in order:
+        leave_third(1, zz).start()
+    for zz in range(DEPTH):
+        for f in range(2):
+            second_third(f, zz).wait_recv()
+    expert(3, 3, (leave.at[0, 1], leave.at[1, 1]))
+    for zz in order:
+        for f in range(2):
+            leave_both(f, zz).start()
+
+    def wide(ref):
+        return ref.astype(jnp.float32)
+
+    def to_second(zz):
+        for f in range(2):
+            leave_both(f, zz).wait_recv()
+            val = pass_on[f, piece(zz), :] + wide(got_third[f, 1, piece(zz), :])
+            got_third[f, 1, piece(zz), :] = val.astype(jnp.bfloat16)
+            leave_second(f, zz).start()
+
+    def settle(zz):
+        for f in range(2):
+            leave_third(f, zz).wait_recv()
+            leave_second(f, zz).wait_recv()
+            stay[f, piece(zz), :] = (
+                stay[f, piece(zz), :]
+                + wide(got_third[f, 0, piece(zz), :])
+                + wide(got_second[f, piece(zz), :])
+            )
+
+        def first_up():
+            for f in range(2):
+                rise[f, piece(zz), :] = stay[f, piece(zz), :].astype(jnp.bfloat16)
+                rising(f, zz).start()
+
+        def first_down():
+            for f in range(2):
+                fall[f, piece(zz), :] = stay[f, piece(zz), :].astype(jnp.bfloat16)
+                falling(f, zz).start()
+
+        if zz > 0:
+            when(z == 0, first_up)
+        if zz < DEPTH - 1:
+            when(z == DEPTH - 1, first_down)
+
+    def relay_up(zz):
+        for f in range(2):
+            rising(f, zz).wait_recv()
+            val = stay[f, piece(zz), :] + wide(rise[f, piece(zz), :])
+            rise[f, piece(zz), :] = val.astype(jnp.bfloat16)
+            rising(f, zz).start()
+
+    def relay_down(zz):
+        for f in range(2):
+            falling(f, zz).wait_recv()
+            val = stay[f, piece(zz), :] + wide(fall[f, piece(zz), :])
+            fall[f, piece(zz), :] = val.astype(jnp.bfloat16)
+            falling(f, zz).start()
+
+    to_second(order[0])
+    for i in range(1, DEPTH + 1):
+        if i < DEPTH:
+            to_second(order[i])
+        settle(order[i - 1])
+        if i == 2:
+            when(z == 1, lambda: relay_up(3))
+            when(z == 2, lambda: relay_down(0))
+        if i == 3:
+            when(z == 1, lambda: relay_down(0))
+            when(z == 2, lambda: relay_up(3))
+    when(z == 1, lambda: relay_up(2))
+    when(z == 2, lambda: relay_down(1))
+
+    cols = (pl.ds(0, half), pl.ds(half, half))
+
+    def finish(up, down):
+        for f in range(2):
+            val = stay[f, piece(z), :]
+            if up:
+                rising(f, z).wait_recv()
+                val = val + wide(rise[f, piece(z), :])
+            if down:
+                falling(f, z).wait_recv()
+                val = val + wide(fall[f, piece(z), :])
+            out_ref[:, cols[f]] = val.astype(out_ref.dtype)
+
+    when(z == 0, lambda: finish(False, True))
+    when(z == DEPTH - 1, lambda: finish(True, False))
+    when(jnp.logical_not(edge), lambda: finish(True, True))
+
+    for _, swap in swaps:
+        swap.wait_send()
+    for f in range(2):
+        for zz in range(DEPTH):
+            when(jnp.logical_and(z < DEPTH - 1, zz <= z), lambda f=f, zz=zz: climb(f, zz).wait_send())
+            when(jnp.logical_and(z > 0, zz >= z), lambda f=f, zz=zz: sink(f, zz).wait_send())
+            for copy in (own_second, own_third, second_third, leave_third, leave_both, leave_second):
+                copy(f, zz).wait_send()
+            when(zz > z, lambda f=f, zz=zz: rising(f, zz).wait_send())
+            when(zz < z, lambda f=f, zz=zz: falling(f, zz).wait_send())
+
+
+def fused_body(tokens, routes, gate_probs, gate_w, up_w, down_w):
+    experts = lax.axis_size("expert")
+    tok, width = tokens.shape
+    unit = gate_w.shape[2]
+    half = width // 2
+    line = DEPTH * tok
+    expert_ids = jnp.arange(experts, dtype=jnp.int32)
+    named = routes[:, :, None] == expert_ids
+    spread = jnp.sum(jnp.where(named, gate_probs[:, :, None], 0.0), axis=1)
+    coarse = lax.reduce_precision(spread, 8, 7)
+    fine = spread - coarse
+    tags = jnp.concatenate([coarse, fine], axis=1).astype(jnp.bfloat16)
+    tags = jnp.pad(tags, ((0, 0), (0, TAG - 2 * experts)))
+    rows = jnp.concatenate([tags, tokens], axis=1)
+    vmem, anywhere = pl.BlockSpec(memory_space=pltpu.VMEM), pl.BlockSpec(memory_space=pl.ANY)
+    bf16, f32, dma = jnp.bfloat16, jnp.float32, pltpu.SemaphoreType.DMA
+    return pl.pallas_call(
+        fused_kernel,
+        out_shape=jax.ShapeDtypeStruct((tok, width), bf16),
+        in_specs=[vmem, anywhere, anywhere, anywhere],
+        out_specs=vmem,
+        scratch_shapes=[
+            pltpu.VMEM((4, line, TAG + half), bf16),
+            pltpu.VMEM((4, line, half), bf16),
+            pltpu.VMEM((width, 4 * unit), bf16),
+            pltpu.VMEM((2 * unit, width), bf16),
+            pltpu.VMEM((line, 2 * unit), bf16),
+            pltpu.VMEM((2, line, half), f32),
+            pltpu.VMEM((2, line, half), f32),
+            pltpu.VMEM((2, 2, line, half), bf16),
+            pltpu.VMEM((2, 2, line, half), bf16),
+            pltpu.VMEM((2, line, half), bf16),
+            pltpu.VMEM((2, line, half), bf16),
+            pltpu.VMEM((2, line, half), bf16),
+            dma((2, 20)),
+            dma((2, 16)),
+            dma((2, 20)),
+            dma((2, 20)),
+            dma((9,)),
+        ],
+        compiler_params=pltpu.CompilerParams(
+            collective_id=0, has_side_effects=True, vmem_limit_bytes=60 * 2**20
+        ),
+        cost_estimate=pl.CostEstimate(
+            flops=2 * experts * tok * width * unit * 6,
+            bytes_accessed=6 * width * unit * 2,
+            transcendentals=experts * tok * unit * 2,
+        ),
+    )(rows, gate_w[0], up_w[0], down_w[0])
+
+
+def body(tokens, routes, *others):
+    tok_count, top_count = routes.shape
+    experts = lax.axis_size("expert")
+    capacity = 2 * tok_count * top_count // experts
+    if capacity >= tok_count and experts == 4 * DEPTH and lax.axis_size("dp") == 2:
+        return fused_body(tokens, routes, *others)
+    return exchange_body(tokens, routes, *others)
+
+
 def solution(mesh):
     return jax.shard_map(
         body,

time: 557 us -> 182 us (0.33); the launches traced: 547 us -> 182 us
  waiting for transfers between devices: 243 us -> 0 us
  blocking collectives: 203 us -> 0 us
  Pallas kernels: 0 us -> 177 us
  matrix products: 49.1 us -> 0 us
  local copies, waits for them, and re-layouts: 19.2 us -> 2.03 us
  between operations: 13.5 us -> 0.02 us
  other arithmetic: 11.9 us -> 2.68 us
  starting transfers between devices: 7.17 us -> 0 us
    all_to_all x2 -> x0, blocking collectives: 203 us -> none  [the longest x1 190 us: body(): lax.all_to_all(outgoing, 'expert', split_axis=0, concat_axis=0, tiled=True)]
    all_to_all x1 -> x0, waiting for transfers between devices: 181 us -> none  [body(): lax.all_to_all(answered, 'expert', split_axis=0, concat_axis=0, tiled=True)]
    pallas_call x0 -> x1, Pallas kernels: none -> 177 us  [fused_body(): pl.pallas_call(fused_kernel, out_shape=jax.ShapeDtypeStruct((tok, width),...]
    dot_general x5 -> x0, matrix products: 49.1 us -> none  [the longest x1 14.5 us: swiglu(): return jnp.dot(hidden, w_down, preferred_element_type=jnp.float32)]
    reduce_scatter x1 -> x0, waiting for transfers between devices: 33.6 us -> none  [body(): lax.psum_scatter(partial_out, 'dp', scatter_dimension=0, tiled=True)]
    all_gather x1 -> x0, waiting for transfers between devices: 28.9 us -> none  [body(): both_rows = lax.all_gather(flat_rows, 'dp', axis=0, tiled=True)]
    gather x6 -> x0, local copies, waits for them, and re-layouts: 17.3 us -> none  [the longest x1 13.2 us: body(): picked = returned.reshape(experts * capacity, model_width)[target]]
    convert_element_type x2 -> x0, other arithmetic: 9.35 us -> none  [the longest x1 9.32 us: body(): masked.astype(jnp.bfloat16).reshape(source_count, item_count, model_width)]
  transfers between devices with their start and end apart: 3 -> 0, of which waited for: 3 -> 0; matrix products, arithmetic and copies ran while one was open for 0% -> 0% of each run, Pallas kernels for 0% -> 0%
where the time goes in v2:
time: 182 us
  Pallas kernels  177 us (97%)
  other arithmetic  2.68 us (1%)
  local copies, waits for them, and re-layouts  2.03 us (1%)
    pallas_call x1, Pallas kernels, fused_body(): pl.pallas_call(fused_kernel, out_shape=jax.ShapeDtypeStruct((tok, width),...  177 us

profile of v2, /device:TPU:8, one launch (start us, length us, event | category | flops | bytes accessed | tf_op | source)
XLA Modules:
  0.0 182.1 jit_solution(12638592161657558911)
XLA Ops:
  0.0 0.7 select_reduce_fusion
  0.7 0.1 copy.12
  0.8 0.1 copy.11
  0.9 0.1 fusion.2
  1.0 1.9 %pad_maximum_fusion.rows_ref = bf16[64,4224]{1,0:T(8,128)(2,1)} fusion(bf16[64,4096]{1,0:T(8,128)(2,1)} %param.6, bf16[64,128]{1,0:T(8,128)(2,1)S(1)} %fusion.2), kind=kLoop, calls=%fused_computation | loop fusion | flops 1081344 | bytes 1081344 | tf_op jit(solution)/shard_map/concatenate | solution.py:396
  2.9 177.3 %shard_map.64 = bf16[64,4096]{1,0:T(8,128)(2,1)} custom-call(bf16[64,4224]{1,0:T(8,128)(2,1)} %pad_maximum_fusion.rows_ref, bf16[4096,384]{1,0:T(8,128)(2,1)} %bitcast.3, bf16[4096,384]{1,0:T(8,128)(2,1)} %bitcast.4, bf16[384,4096]{1,0:T(8,128)(2,1)} %bitcast.5), custom_call_target="tpu_custom_call" | custom-call | flops 19327352832 | bytes 18874368 | tf_op jit(solution)/shard_map/pallas_call | solution.py:399
  180.2 1.9 %copy.15 = bf16[64,4096]{1,0:T(8,128)(2,1)} copy(bf16[64,4096]{1,0:T(8,128)(2,1)} %shard_map.64) | data formatting | bytes 1048576
  (2 shorter events, 0.0 us)

commit v3 on v2

--- a/solution.py
+++ b/solution.py
@@ -64,7 +64,7 @@
 
 
 def fused_kernel(
-    rows_ref, gate_ref, up_ref, down_ref, out_ref,
+    rows_ref, routes_ref, probs_ref, gate_ref, up_ref, down_ref, out_ref,
     xa, xb, w_in, w_out, hidden, stay, pass_on, leave, got_third, got_second, rise, fall,
     gather_send, gather_recv, reduce_send, reduce_recv, weight_sem,
 ):
@@ -109,8 +109,16 @@
     def _():
         pl.semaphore_signal(barrier, inc=1, device_id=below, device_id_type=MESH)
 
-    xa[0, piece(z), :] = rows_ref[:, : TAG + half]
-    xb[0, piece(z), :] = rows_ref[:, TAG + half :]
+    tag_lane = lax.broadcasted_iota(jnp.int32, (tok, TAG), 1)
+    spread = jnp.zeros((tok, TAG), jnp.float32)
+    for k in range(routes_ref.shape[1]):
+        named = (tag_lane & 15) == routes_ref[:, k : k + 1]
+        spread = spread + jnp.where(named, probs_ref[:, k : k + 1], 0.0)
+    coarse = spread.astype(jnp.bfloat16).astype(jnp.float32)
+    tags_own = jnp.where(tag_lane < 16, coarse, spread - coarse)
+    xa[0, piece(z), :TAG] = tags_own.astype(jnp.bfloat16)
+    xa[0, piece(z), TAG:] = rows_ref[:, :half]
+    xb[0, piece(z), :] = rows_ref[:, half:]
 
     edge = jnp.logical_or(z == 0, z == DEPTH - 1)
 
@@ -168,6 +176,17 @@
             own_second(f, zz).wait_recv()
             second_third(f, zz).start()
 
+    def send_third(zz):
+        for f in range(2):
+            own_third(f, zz).start()
+
+    def at_stage(k, fn):
+        if k == 0:
+            fn(z)
+        else:
+            when(z >= k, lambda: fn(z - k))
+            when(z + k < DEPTH, lambda: fn(z + k))
+
     for k in range(1, DEPTH):
         def from_below(k=k):
             zz = z - k
@@ -175,7 +194,6 @@
                 climb(f, zz).wait_recv()
                 when(z < DEPTH - 1, lambda f=f: climb(f, zz).start())
                 own_second(f, zz).start()
-                own_third(f, zz).start()
 
         def from_above(k=k):
             zz = z + k
@@ -183,15 +201,12 @@
                 sink(f, zz).wait_recv()
                 when(z > 0, lambda f=f: sink(f, zz).start())
                 own_second(f, zz).start()
-                own_third(f, zz).start()
 
         when(z >= k, from_below)
         when(z + k < DEPTH, from_above)
-        if k == 1:
-            relay_second(z)
-        else:
-            when(z >= k - 1, lambda k=k: relay_second(z - k + 1))
-            when(z + k - 1 < DEPTH, lambda k=k: relay_second(z + k - 1))
+        at_stage(k - 1, relay_second)
+        if k == 2:
+            at_stage(1, send_third)
 
     def expert(kind_a, kind_b, targets):
         lane = lax.broadcasted_iota(jnp.int32, (DEPTH * tok, TAG), 1)
@@ -267,36 +282,44 @@
         local.wait()
         swap.wait_recv()
     expert(0, 0, (stay.at[0], stay.at[1]))
-    when(z >= 3, lambda: relay_second(z - 3))
-    when(z + 3 < DEPTH, lambda: relay_second(z + 3))
+    at_stage(3, relay_second)
+    at_stage(2, send_third)
+    at_stage(3, send_third)
+
+    def wide(ref):
+        return ref.astype(jnp.float32)
+
+    def to_second(f, zz):
+        leave_both(f, zz).wait_recv()
+        val = pass_on[f, piece(zz), :] + wide(got_third[f, 1, piece(zz), :])
+        got_third[f, 1, piece(zz), :] = val.astype(jnp.bfloat16)
+        leave_second(f, zz).start()
+
+    for zz in range(DEPTH):
+        for f in range(2):
+            second_third(f, zz).wait_recv()
+    expert(3, 3, (leave.at[0, 1], leave.at[1, 1]))
+    for zz in order:
+        for f in range(2):
+            leave_both(f, zz).start()
 
     for zz in range(DEPTH):
         own_third(0, zz).wait_recv()
     expert(2, 1, (leave.at[0, 0], pass_on.at[1]))
+    for zz in order[:2]:
+        to_second(1, zz)
     for zz in order:
         leave_third(0, zz).start()
     for zz in range(DEPTH):
         own_third(1, zz).wait_recv()
     expert(1, 2, (pass_on.at[0], leave.at[1, 0]))
+    for zz in order[:2]:
+        to_second(0, zz)
     for zz in order:
         leave_third(1, zz).start()
-    for zz in range(DEPTH):
-        for f in range(2):
-            second_third(f, zz).wait_recv()
-    expert(3, 3, (leave.at[0, 1], leave.at[1, 1]))
-    for zz in order:
-        for f in range(2):
-            leave_both(f, zz).start()
-
-    def wide(ref):
-        return ref.astype(jnp.float32)
-
-    def to_second(zz):
-        for f in range(2):
-            leave_both(f, zz).wait_recv()
-            val = pass_on[f, piece(zz), :] + wide(got_third[f, 1, piece(zz), :])
-            got_third[f, 1, piece(zz), :] = val.astype(jnp.bfloat16)
-            leave_second(f, zz).start()
+    for zz in order[2:]:
+        for f in range(2):
+            to_second(f, zz)
 
     def settle(zz):
         for f in range(2):
@@ -337,10 +360,7 @@
             fall[f, piece(zz), :] = val.astype(jnp.bfloat16)
             falling(f, zz).start()
 
-    to_second(order[0])
     for i in range(1, DEPTH + 1):
-        if i < DEPTH:
-            to_second(order[i])
         settle(order[i - 1])
         if i == 2:
             when(z == 1, lambda: relay_up(3))
@@ -386,20 +406,12 @@
     unit = gate_w.shape[2]
     half = width // 2
     line = DEPTH * tok
-    expert_ids = jnp.arange(experts, dtype=jnp.int32)
-    named = routes[:, :, None] == expert_ids
-    spread = jnp.sum(jnp.where(named, gate_probs[:, :, None], 0.0), axis=1)
-    coarse = lax.reduce_precision(spread, 8, 7)
-    fine = spread - coarse
-    tags = jnp.concatenate([coarse, fine], axis=1).astype(jnp.bfloat16)
-    tags = jnp.pad(tags, ((0, 0), (0, TAG - 2 * experts)))
-    rows = jnp.concatenate([tags, tokens], axis=1)
     vmem, anywhere = pl.BlockSpec(memory_space=pltpu.VMEM), pl.BlockSpec(memory_space=pl.ANY)
     bf16, f32, dma = jnp.bfloat16, jnp.float32, pltpu.SemaphoreType.DMA
     return pl.pallas_call(
         fused_kernel,
         out_shape=jax.ShapeDtypeStruct((tok, width), bf16),
-        in_specs=[vmem, anywhere, anywhere, anywhere],
+        in_specs=[vmem, vmem, vmem, anywhere, anywhere, anywhere],
         out_specs=vmem,
         scratch_shapes=[
             pltpu.VMEM((4, line, TAG + half), bf16),
@@ -428,7 +440,7 @@
             bytes_accessed=6 * width * unit * 2,
             transcendentals=experts * tok * unit * 2,
         ),
-    )(rows, gate_w[0], up_w[0], down_w[0])
+    )(tokens, routes, gate_probs, gate_w[0], up_w[0], down_w[0])
 
 
 def body(tokens, routes, *others):

time: 182 us -> 172 us (0.945)
  Pallas kernels: 177 us -> 167 us
  other arithmetic: 2.68 us -> 0 us
  local copies, waits for them, and re-layouts: 2.03 us -> 4.62 us
    pallas_call x1, Pallas kernels: 177 us -> 167 us  [fused_body(): pl.pallas_call(fused_kernel, out_shape=jax.ShapeDtypeStruct((tok, width),...]
    unnamed x1 -> x3, local copies, waits for them, and re-layouts: 1.87 us -> 4.62 us
    concatenate x2 -> x0, other arithmetic: 1.95 us -> none  [the longest x1 1.87 us: fused_body(): rows = jnp.concatenate([tags, tokens], axis=1)]
where the time goes in v3:
time: 172 us
  Pallas kernels  167 us (97%)
  local copies, waits for them, and re-layouts  4.62 us (3%)
    pallas_call x1, Pallas kernels, fused_body(): pl.pallas_call(fused_kernel, out_shape=jax.ShapeDtypeStruct((tok, width),...  167 us
    unnamed x3, local copies, waits for them, and re-layouts  4.62 us

profile of v3, /device:TPU:8, one launch (start us, length us, event | category | flops | bytes accessed | tf_op | source)
XLA Modules:
  0.0 172.0 jit_solution(15689339250879902843)
XLA Ops:
  0.0 1.4 copy.7.routes_ref
  1.4 1.4 copy.8.probs_ref
  2.8 167.3 %shard_map.64 = bf16[64,4096]{1,0:T(8,128)(2,1)} custom-call(bf16[64,4096]{1,0:T(8,128)(2,1)} %rows_ref.1, s32[64,8]{1,0:T(8,128)} %copy.7.routes_ref, f32[64,8]{1,0:T(8,128)} %copy.8.probs_ref, bf16[4096,384]{1,0:T(8,128)(2,1)} %bitcast.3, bf16[4096,384]{1,0:T(8,128)(2,1)} %bitcast.4, bf16[384,4096]{1,0:T(8,128)(2,1)} %bitcast.5), custom_call_target="tpu_custom_call" | custom-call | flops 19327352832 | bytes 18874368 | tf_op jit(solution)/shard_map/pallas_call | solution.py:411
  170.1 1.9 %copy.10 = bf16[64,4096]{1,0:T(8,128)(2,1)} copy(bf16[64,4096]{1,0:T(8,128)(2,1)} %shard_map.64) | data formatting | bytes 1048576

commit v4 on v3

--- a/solution.py
+++ b/solution.py
@@ -64,8 +64,8 @@
 
 
 def fused_kernel(
-    rows_ref, routes_ref, probs_ref, gate_ref, up_ref, down_ref, out_ref,
-    xa, xb, w_in, w_out, hidden, stay, pass_on, leave, got_third, got_second, rise, fall,
+    rows_ref, tags_ref, gate_ref, up_ref, down_ref, out_ref,
+    xa, xb, w_in, w_out, hidden, stay, pass_on, leave, got_third, got_second, rise, fall, early_rise, early_fall,
     gather_send, gather_recv, reduce_send, reduce_recv, weight_sem,
 ):
     tok = rows_ref.shape[0]
@@ -82,6 +82,10 @@
     second = (across_y, across_x)
     third = (across_x, across_y)
     feats = (xa, xb)
+    quarter = half // 2
+    left_cols, right_cols = pl.ds(0, quarter), pl.ds(quarter, quarter)
+    left = (pl.ds(0, TAG + quarter), left_cols)
+    right = (pl.ds(TAG + quarter, quarter), right_cols)
 
     def when(cond, fn):
         pl.when(cond)(fn)
@@ -109,14 +113,7 @@
     def _():
         pl.semaphore_signal(barrier, inc=1, device_id=below, device_id_type=MESH)
 
-    tag_lane = lax.broadcasted_iota(jnp.int32, (tok, TAG), 1)
-    spread = jnp.zeros((tok, TAG), jnp.float32)
-    for k in range(routes_ref.shape[1]):
-        named = (tag_lane & 15) == routes_ref[:, k : k + 1]
-        spread = spread + jnp.where(named, probs_ref[:, k : k + 1], 0.0)
-    coarse = spread.astype(jnp.bfloat16).astype(jnp.float32)
-    tags_own = jnp.where(tag_lane < 16, coarse, spread - coarse)
-    xa[0, piece(z), :TAG] = tags_own.astype(jnp.bfloat16)
+    xa[0, piece(z), :TAG] = tags_ref[...]
     xa[0, piece(z), TAG:] = rows_ref[:, :half]
     xb[0, piece(z), :] = rows_ref[:, half:]
 
@@ -149,7 +146,28 @@
         return gather(f, 0, 2, zz, 12, third[f])
 
     def second_third(f, zz):
-        return gather(f, 1, 3, zz, 16, third[f])
+        return remote(
+            feats[f].at[1, piece(zz), left[f]], feats[f].at[3, piece(zz), left[f]],
+            gather_send.at[f, 16 + zz], gather_recv.at[f, 12 + zz], third[f],
+        )
+
+    def right_third(f):
+        return remote(
+            feats[f].at[1, piece(z), right[f]], feats[f].at[3, piece(z), right[f]],
+            gather_send.at[f, 28], gather_recv.at[f, 16 + z], third[f],
+        )
+
+    def right_line(f, zz, slot, device):
+        ref = feats[f].at[3, piece(zz), right[f]]
+        return remote(
+            ref, ref, gather_send.at[f, slot + zz], gather_recv.at[f, 16 + zz], device
+        )
+
+    def right_climb(f, zz):
+        return right_line(f, zz, 20, above)
+
+    def right_sink(f, zz):
+        return right_line(f, zz, 24, below)
 
     for f in range(2):
         when(z < DEPTH - 1, lambda f=f: climb(f, z).start())
@@ -187,6 +205,20 @@
             when(z >= k, lambda: fn(z - k))
             when(z + k < DEPTH, lambda: fn(z + k))
 
+    def relay_right(k):
+        def from_below():
+            for f in range(2):
+                right_climb(f, z - k).wait_recv()
+                when(z < DEPTH - 1, lambda f=f: right_climb(f, z - k).start())
+
+        def from_above():
+            for f in range(2):
+                right_sink(f, z + k).wait_recv()
+                when(z > 0, lambda f=f: right_sink(f, z + k).start())
+
+        when(z >= k, from_below)
+        when(z + k < DEPTH, from_above)
+
     for k in range(1, DEPTH):
         def from_below(k=k):
             zz = z - k
@@ -205,8 +237,17 @@
         when(z >= k, from_below)
         when(z + k < DEPTH, from_above)
         at_stage(k - 1, relay_second)
+        if k == 1:
+            for f in range(2):
+                right_third(f).start()
         if k == 2:
+            for f in range(2):
+                right_third(f).wait_recv()
+                when(z < DEPTH - 1, lambda f=f: right_climb(f, z).start())
+                when(z > 0, lambda f=f: right_sink(f, z).start())
             at_stage(1, send_third)
+        if k == 3:
+            relay_right(1)
 
     def expert(kind_a, kind_b, targets):
         lane = lax.broadcasted_iota(jnp.int32, (DEPTH * tok, TAG), 1)
@@ -256,9 +297,23 @@
 
     def leave_both(f, zz):
         return remote(
-            leave.at[f, 1, piece(zz)], got_third.at[f, 1, piece(zz)],
+            leave.at[f, 1, piece(zz), left_cols], got_third.at[f, 1, piece(zz), left_cols],
             reduce_send.at[f, 4 + zz], reduce_recv.at[f, 4 + zz], third[f],
         )
+
+    def leave_right(f):
+        return remote(
+            leave.at[f, 1, piece(z), right_cols], got_third.at[f, 1, piece(z), right_cols],
+            reduce_send.at[f, 28], reduce_recv.at[f, 28], third[f],
+        )
+
+    def early_rising(f, zz):
+        ref = early_rise.at[f, piece(zz)]
+        return remote(ref, ref, reduce_send.at[f, 20 + zz], reduce_recv.at[f, 20 + zz], above)
+
+    def early_falling(f, zz):
+        ref = early_fall.at[f, piece(zz)]
+        return remote(ref, ref, reduce_send.at[f, 24 + zz], reduce_recv.at[f, 24 + zz], below)
 
     def leave_second(f, zz):
         return remote(
@@ -282,6 +337,7 @@
         local.wait()
         swap.wait_recv()
     expert(0, 0, (stay.at[0], stay.at[1]))
+    relay_right(2)
     at_stage(3, relay_second)
     at_stage(2, send_third)
     at_stage(3, send_third)
@@ -290,22 +346,71 @@
         return ref.astype(jnp.float32)
 
     def to_second(f, zz):
-        leave_both(f, zz).wait_recv()
-        val = pass_on[f, piece(zz), :] + wide(got_third[f, 1, piece(zz), :])
-        got_third[f, 1, piece(zz), :] = val.astype(jnp.bfloat16)
-        leave_second(f, zz).start()
+        def go():
+            leave_both(f, zz).wait_recv()
+            val = pass_on[f, piece(zz), left_cols] + wide(got_third[f, 1, piece(zz), left_cols])
+            got_third[f, 1, piece(zz), left_cols] = val.astype(jnp.bfloat16)
+            got_third[f, 1, piece(zz), right_cols] = pass_on[f, piece(zz), right_cols].astype(
+                jnp.bfloat16
+            )
+            leave_second(f, zz).start()
+
+        when(zz != z, go)
+
+    def own_to_second(f):
+        leave_both(f, z).wait_recv()
+        leave_right(f).wait_recv()
+        val = pass_on[f, piece(z), :] + wide(got_third[f, 1, piece(z), :])
+        got_third[f, 1, piece(z), :] = val.astype(jnp.bfloat16)
+        leave_second(f, z).start()
+
+    def early_relay(buf, copy, zz):
+        for f in range(2):
+            copy(f, zz).wait_recv()
+            val = wide(leave[f, 1, piece(zz), right_cols]) + wide(buf[f, piece(zz), :])
+            buf[f, piece(zz), :] = val.astype(jnp.bfloat16)
+            copy(f, zz).start()
+
+    def early_up(zz):
+        early_relay(early_rise, early_rising, zz)
+
+    def early_down(zz):
+        early_relay(early_fall, early_falling, zz)
+
+    def early_first(buf, copy, pieces):
+        for zz in pieces:
+            for f in range(2):
+                buf[f, piece(zz), :] = leave[f, 1, piece(zz), right_cols]
+                copy(f, zz).start()
+
+    def early_finish(up, down):
+        for f in range(2):
+            val = wide(leave[f, 1, piece(z), right_cols])
+            if up:
+                early_rising(f, z).wait_recv()
+                val = val + wide(early_rise[f, piece(z), :])
+            if down:
+                early_falling(f, z).wait_recv()
+                val = val + wide(early_fall[f, piece(z), :])
+            leave[f, 1, piece(z), right_cols] = val.astype(jnp.bfloat16)
+            leave_right(f).start()
 
     for zz in range(DEPTH):
         for f in range(2):
             second_third(f, zz).wait_recv()
+    relay_right(3)
     expert(3, 3, (leave.at[0, 1], leave.at[1, 1]))
     for zz in order:
         for f in range(2):
             leave_both(f, zz).start()
+    when(z == 0, lambda: early_first(early_rise, early_rising, (3, 2, 1)))
+    when(z == DEPTH - 1, lambda: early_first(early_fall, early_falling, (0, 1, 2)))
 
     for zz in range(DEPTH):
         own_third(0, zz).wait_recv()
     expert(2, 1, (leave.at[0, 0], pass_on.at[1]))
+    when(z == 1, lambda: early_up(3))
+    when(z == 2, lambda: early_down(0))
     for zz in order[:2]:
         to_second(1, zz)
     for zz in order:
@@ -313,13 +418,20 @@
     for zz in range(DEPTH):
         own_third(1, zz).wait_recv()
     expert(1, 2, (pass_on.at[0], leave.at[1, 0]))
+    when(z == 1, lambda: early_down(0))
+    when(z == 2, lambda: early_up(3))
     for zz in order[:2]:
         to_second(0, zz)
     for zz in order:
         leave_third(1, zz).start()
+    when(z == 1, lambda: early_up(2))
+    when(z == 2, lambda: early_down(1))
     for zz in order[2:]:
         for f in range(2):
             to_second(f, zz)
+    when(z == 0, lambda: early_finish(False, True))
+    when(z == DEPTH - 1, lambda: early_finish(True, False))
+    when(jnp.logical_not(edge), lambda: early_finish(True, True))
 
     def settle(zz):
         for f in range(2):
@@ -341,6 +453,8 @@
                 fall[f, piece(zz), :] = stay[f, piece(zz), :].astype(jnp.bfloat16)
                 falling(f, zz).start()
 
+        if not isinstance(zz, int):
+            return
         if zz > 0:
             when(z == 0, first_up)
         if zz < DEPTH - 1:
@@ -361,8 +475,10 @@
             falling(f, zz).start()
 
     for i in range(1, DEPTH + 1):
-        settle(order[i - 1])
+        when(z != order[i - 1], lambda i=i: settle(order[i - 1]))
         if i == 2:
+            for f in range(2):
+                own_to_second(f)
             when(z == 1, lambda: relay_up(3))
             when(z == 2, lambda: relay_down(0))
         if i == 3:
@@ -371,6 +487,7 @@
     when(z == 1, lambda: relay_up(2))
     when(z == 2, lambda: relay_down(1))
 
+    settle(z)
     cols = (pl.ds(0, half), pl.ds(half, half))
 
     def finish(up, down):
@@ -398,6 +515,12 @@
                 copy(f, zz).wait_send()
             when(zz > z, lambda f=f, zz=zz: rising(f, zz).wait_send())
             when(zz < z, lambda f=f, zz=zz: falling(f, zz).wait_send())
+            when(zz > z, lambda f=f, zz=zz: early_rising(f, zz).wait_send())
+            when(zz < z, lambda f=f, zz=zz: early_falling(f, zz).wait_send())
+            when(jnp.logical_and(z < DEPTH - 1, zz <= z), lambda f=f, zz=zz: right_climb(f, zz).wait_send())
+            when(jnp.logical_and(z > 0, zz >= z), lambda f=f, zz=zz: right_sink(f, zz).wait_send())
+        right_third(f).wait_send()
+        leave_right(f).wait_send()
 
 
 def fused_body(tokens, routes, gate_probs, gate_w, up_w, down_w):
@@ -406,12 +529,19 @@
     unit = gate_w.shape[2]
     half = width // 2
     line = DEPTH * tok
+    expert_ids = jnp.arange(experts, dtype=jnp.int32)
+    named = routes[:, :, None] == expert_ids
+    spread = jnp.sum(jnp.where(named, gate_probs[:, :, None], 0.0), axis=1)
+    coarse = lax.reduce_precision(spread, 8, 7)
+    fine = spread - coarse
+    tags = jnp.concatenate([coarse, fine], axis=1).astype(jnp.bfloat16)
+    tags = jnp.pad(tags, ((0, 0), (0, TAG - 2 * experts)))
     vmem, anywhere = pl.BlockSpec(memory_space=pltpu.VMEM), pl.BlockSpec(memory_space=pl.ANY)
     bf16, f32, dma = jnp.bfloat16, jnp.float32, pltpu.SemaphoreType.DMA
     return pl.pallas_call(
         fused_kernel,
         out_shape=jax.ShapeDtypeStruct((tok, width), bf16),
-        in_specs=[vmem, vmem, vmem, anywhere, anywhere, anywhere],
+        in_specs=[vmem, vmem, anywhere, anywhere, anywhere],
         out_specs=vmem,
         scratch_shapes=[
             pltpu.VMEM((4, line, TAG + half), bf16),
@@ -426,10 +556,12 @@
             pltpu.VMEM((2, line, half), bf16),
             pltpu.VMEM((2, line, half), bf16),
             pltpu.VMEM((2, line, half), bf16),
+            pltpu.VMEM((2, line, half // 2), bf16),
+            pltpu.VMEM((2, line, half // 2), bf16),
+            dma((2, 29)),
             dma((2, 20)),
-            dma((2, 16)),
-            dma((2, 20)),
-            dma((2, 20)),
+            dma((2, 29)),
+            dma((2, 29)),
             dma((9,)),
         ],
         compiler_params=pltpu.CompilerParams(
@@ -440,7 +572,7 @@
             bytes_accessed=6 * width * unit * 2,
             transcendentals=experts * tok * unit * 2,
         ),
-    )(tokens, routes, gate_probs, gate_w[0], up_w[0], down_w[0])
+    )(tokens, tags, gate_w[0], up_w[0], down_w[0])
 
 
 def body(tokens, routes, *others):

time: 172 us -> 156 us (0.907)
  Pallas kernels: 167 us -> 152 us
  local copies, waits for them, and re-layouts: 4.62 us -> 2.03 us
    pallas_call x1, Pallas kernels: 167 us -> 152 us  [fused_body(): pl.pallas_call(fused_kernel, out_shape=jax.ShapeDtypeStruct((tok, width),...]
    unnamed x3 -> x1, local copies, waits for them, and re-layouts: 4.62 us -> 1.87 us
where the time goes in v4:
time: 156 us; the launch traced here: 155 us
  Pallas kernels  152 us (97%)
  local copies, waits for them, and re-layouts  2.03 us (1%)
    pallas_call x1, Pallas kernels, fused_body(): pl.pallas_call(fused_kernel, out_shape=jax.ShapeDtypeStruct((tok, width),...  152 us

profile of v4, /device:TPU:8, one launch (start us, length us, event | category | flops | bytes accessed | tf_op | source)
XLA Modules:
  0.0 155.4 jit_solution(14746598808897269953)
XLA Ops:
  0.0 0.7 select_reduce_fusion
  0.7 0.1 copy.12
  0.8 0.1 copy.11
  0.9 0.7 fusion.2.tags_ref
  1.6 151.9 %shard_map.64 = bf16[64,4096]{1,0:T(8,128)(2,1)} custom-call(bf16[64,4096]{1,0:T(8,128)(2,1)} %rows_ref.1, bf16[64,128]{1,0:T(8,128)(2,1)} %fusion.2.tags_ref, bf16[4096,384]{1,0:T(8,128)(2,1)} %bitcast.3, bf16[4096,384]{1,0:T(8,128)(2,1)} %bitcast.4, bf16[384,4096]{1,0:T(8,128)(2,1)} %bitcast.5), custom_call_target="tpu_custom_call" | custom-call | flops 19327352832 | bytes 18874368 | tf_op jit(solution)/shard_map/pallas_call | solution.py:541
  153.5 1.9 %copy.15 = bf16[64,4096]{1,0:T(8,128)(2,1)} copy(bf16[64,4096]{1,0:T(8,128)(2,1)} %shard_map.64) | data formatting | bytes 1048576
  (2 shorter events, 0.0 us)

commit v5 on v4

--- a/solution.py
+++ b/solution.py
@@ -195,8 +195,7 @@
             second_third(f, zz).start()
 
     def send_third(zz):
-        for f in range(2):
-            own_third(f, zz).start()
+        own_third(0, zz).start()
 
     def at_stage(k, fn):
         if k == 0:
@@ -226,6 +225,7 @@
                 climb(f, zz).wait_recv()
                 when(z < DEPTH - 1, lambda f=f: climb(f, zz).start())
                 own_second(f, zz).start()
+            own_third(1, zz).start()
 
         def from_above(k=k):
             zz = z + k
@@ -233,6 +233,7 @@
                 sink(f, zz).wait_recv()
                 when(z > 0, lambda f=f: sink(f, zz).start())
                 own_second(f, zz).start()
+            own_third(1, zz).start()
 
         when(z >= k, from_below)
         when(z + k < DEPTH, from_above)
@@ -396,6 +397,11 @@
             leave_right(f).start()
 
     for zz in range(DEPTH):
+        own_third(1, zz).wait_recv()
+    expert(1, 2, (pass_on.at[0], leave.at[1, 0]))
+    for zz in order[:2]:
+        leave_third(1, zz).start()
+    for zz in range(DEPTH):
         for f in range(2):
             second_third(f, zz).wait_recv()
     relay_right(3)
@@ -405,30 +411,28 @@
             leave_both(f, zz).start()
     when(z == 0, lambda: early_first(early_rise, early_rising, (3, 2, 1)))
     when(z == DEPTH - 1, lambda: early_first(early_fall, early_falling, (0, 1, 2)))
+    for zz in order[2:]:
+        leave_third(1, zz).start()
 
     for zz in range(DEPTH):
         own_third(0, zz).wait_recv()
     expert(2, 1, (leave.at[0, 0], pass_on.at[1]))
+    for zz in order[:2]:
+        leave_third(0, zz).start()
     when(z == 1, lambda: early_up(3))
     when(z == 2, lambda: early_down(0))
     for zz in order[:2]:
-        to_second(1, zz)
-    for zz in order:
+        for f in range(2):
+            to_second(f, zz)
+    for zz in order[2:]:
         leave_third(0, zz).start()
-    for zz in range(DEPTH):
-        own_third(1, zz).wait_recv()
-    expert(1, 2, (pass_on.at[0], leave.at[1, 0]))
     when(z == 1, lambda: early_down(0))
     when(z == 2, lambda: early_up(3))
-    for zz in order[:2]:
-        to_second(0, zz)
-    for zz in order:
-        leave_third(1, zz).start()
+    for zz in order[2:]:
+        for f in range(2):
+            to_second(f, zz)
     when(z == 1, lambda: early_up(2))
     when(z == 2, lambda: early_down(1))
-    for zz in order[2:]:
-        for f in range(2):
-            to_second(f, zz)
     when(z == 0, lambda: early_finish(False, True))
     when(z == DEPTH - 1, lambda: early_finish(True, False))
     when(jnp.logical_not(edge), lambda: early_finish(True, True))

time: 156 us -> 165 us (1.058)
  Pallas kernels: 152 us -> 161 us
    pallas_call x1, Pallas kernels: 152 us -> 161 us  [fused_body(): pl.pallas_call(fused_kernel, out_shape=jax.ShapeDtypeStruct((tok, width),...]
where the time goes in v5:
time: 165 us
  Pallas kernels  161 us (98%)
  local copies, waits for them, and re-layouts  2.03 us (1%)
    pallas_call x1, Pallas kernels, fused_body(): pl.pallas_call(fused_kernel, out_shape=jax.ShapeDtypeStruct((tok, width),...  161 us

profile of v5, /device:TPU:8, one launch (start us, length us, event | category | flops | bytes accessed | tf_op | source)
XLA Modules:
  0.0 164.7 jit_solution(18281740103637227260)
XLA Ops:
  0.0 0.7 select_reduce_fusion
  0.7 0.1 copy.12
  0.8 0.1 copy.11
  0.9 0.7 fusion.2.tags_ref
  1.6 161.3 %shard_map.64 = bf16[64,4096]{1,0:T(8,128)(2,1)} custom-call(bf16[64,4096]{1,0:T(8,128)(2,1)} %rows_ref.1, bf16[64,128]{1,0:T(8,128)(2,1)} %fusion.2.tags_ref, bf16[4096,384]{1,0:T(8,128)(2,1)} %bitcast.3, bf16[4096,384]{1,0:T(8,128)(2,1)} %bitcast.4, bf16[384,4096]{1,0:T(8,128)(2,1)} %bitcast.5), custom_call_target="tpu_custom_call" | custom-call | flops 19327352832 | bytes 18874368 | tf_op jit(solution)/shard_map/pallas_call | solution.py:545
  162.9 1.9 %copy.15 = bf16[64,4096]{1,0:T(8,128)(2,1)} copy(bf16[64,4096]{1,0:T(8,128)(2,1)} %shard_map.64) | data formatting | bytes 1048576
  (2 shorter events, 0.0 us)

commit v6 on v4

--- a/solution.py
+++ b/solution.py
@@ -333,14 +333,14 @@
             reduce_send.at[f, 16 + zz], reduce_recv.at[f, 16 + zz], below,
         )
 
+    relay_right(2)
+    at_stage(3, relay_second)
+    at_stage(2, send_third)
+    at_stage(3, send_third)
     for local, swap in swaps:
         local.wait()
         swap.wait_recv()
     expert(0, 0, (stay.at[0], stay.at[1]))
-    relay_right(2)
-    at_stage(3, relay_second)
-    at_stage(2, send_third)
-    at_stage(3, send_third)
 
     def wide(ref):
         return ref.astype(jnp.float32)

time: 156 us -> 156 us (level)
  no operation moved by 1% of the time
where the time goes in v6:
time: 156 us
  Pallas kernels  153 us (98%)
  local copies, waits for them, and re-layouts  2.03 us (1%)
    pallas_call x1, Pallas kernels, fused_body(): pl.pallas_call(fused_kernel, out_shape=jax.ShapeDtypeStruct((tok, width),...  153 us

profile of v6, /device:TPU:8, one launch (start us, length us, event | category | flops | bytes accessed | tf_op | source)
XLA Modules:
  0.0 156.1 jit_solution(1900190079649834542)
XLA Ops:
  0.0 0.7 select_reduce_fusion
  0.7 0.1 copy.12
  0.8 0.1 copy.11
  0.9 0.7 fusion.2.tags_ref
  1.6 152.7 %shard_map.64 = bf16[64,4096]{1,0:T(8,128)(2,1)} custom-call(bf16[64,4096]{1,0:T(8,128)(2,1)} %rows_ref.1, bf16[64,128]{1,0:T(8,128)(2,1)} %fusion.2.tags_ref, bf16[4096,384]{1,0:T(8,128)(2,1)} %bitcast.3, bf16[4096,384]{1,0:T(8,128)(2,1)} %bitcast.4, bf16[384,4096]{1,0:T(8,128)(2,1)} %bitcast.5), custom_call_target="tpu_custom_call" | custom-call | flops 19327352832 | bytes 18874368 | tf_op jit(solution)/shard_map/pallas_call | solution.py:541
  154.3 1.9 %copy.15 = bf16[64,4096]{1,0:T(8,128)(2,1)} copy(bf16[64,4096]{1,0:T(8,128)(2,1)} %shard_map.64) | data formatting | bytes 1048576
  (2 shorter events, 0.0 us)
